TPU v7x, 32 devices: a whole 2x2x4 slice. The times are simulated.
32 devices in a mesh: row: 4 (over z), col: 8 (over y, x, core).
Axes of the slice: x: 2, y: 2, z: 4, core: 2. Of those that a mesh axis runs over, the one named last changes fastest.
Arguments:
- slots: bfloat16 [192, 128, 128], P(('row', 'col')), may hold values from -6 to 6
- block_list: int32 [192], P(('row', 'col')), may hold values from -1 to 63, as said below
- metric: bfloat16 [8192, 1024], P('row', 'col'), may hold values from -0.125 to 0.125
Outputs:
- contracted: float32 [4096, 1024], P('row', 'col')
Inputs may be any that keep to these rules, and one draw needn't show every extreme that they name: `block_list`: the live entries of one device's 6 slots come first and name distinct blocks; -1 marks an unused slot; every device has at least 3 live slots and some device has all 6 live.
All inputs are finite; a program needn't handle non-finite values.
Results may differ from a plain program's by a relative error of at most 0.0003.
Values may be sent and summed in bfloat16 or wider, within the bound.
A program may use at most 128 MiB of HBM per device.

v0:
```python
import jax
import jax.numpy as jnp
from jax import lax
from jax.sharding import PartitionSpec as P

BLK = 128
PAIR_DEV = 1024


def on_device(slots, block_list, metric):
    slot_count = block_list.shape[0]
    width = slots.shape[1]
    out_cols = metric.shape[1]
    metric_band = lax.all_gather(metric, "row", axis=0, tiled=True)
    band_blocks = metric_band.shape[0] // width
    col_blocks = band_blocks // lax.axis_size("col")
    pair_blocks = PAIR_DEV // BLK
    metric_blocks = metric_band.reshape(band_blocks, width, out_cols)
    piece_slots = lax.all_gather(slots, "col", axis=0, tiled=True)
    piece_list = lax.all_gather(block_list, "col", axis=0, tiled=True)
    number = piece_list.shape[0]
    shard_of = jnp.arange(number, dtype=jnp.int32) // slot_count
    is_live = piece_list >= 0
    clipped = jnp.maximum(piece_list, 0)
    pair_block = clipped // col_blocks
    global_block = shard_of * col_blocks + clipped % col_blocks
    rows = metric_blocks[global_block]
    prod = jnp.einsum("sab,sbq->saq", piece_slots, rows, preferred_element_type=jnp.float32)
    placing = ((pair_block[:, None] == jnp.arange(pair_blocks)[None, :]) & is_live[:, None]).astype(
        jnp.float32
    )
    added = jnp.einsum("sp,saq->paq", placing, prod, precision=lax.Precision.HIGHEST)
    return added.reshape(pair_blocks * width, out_cols)


def solution(mesh):
    return jax.shard_map(
        on_device,
        mesh=mesh,
        in_specs=(P(("row", "col"), None, None), P(("row", "col")), P("row", "col")),
        out_specs=P("row", "col"),
        check_vma=False,
    )
```

profile of v0, /device:TPU:0, one launch (start us, length us, event | category | flops | bytes accessed | tf_op | source)
XLA Modules:
  0.0 99.7 jit_solution(3443984128802064456)
XLA Ops:
  6.5 0.0 all-gather.3.cloned.1.call-start
  6.5 0.7 all-gather.3.cloned.1.call-update
  7.3 0.0 all-gather.5.cloned.1.call-start
  7.3 0.7 all-gather.5.cloned.1.call-update
  8.0 1.2 %dynamic-slice = u32[1]{0:T(128)} dynamic-slice(u32[32]{0:T(128)} %constant.45, u32[]{:T(128)S(6)} %add.21), dynamic_slice_sizes={1} | dynamic-slice | bytes 12
  9.9 0.9 dynamic-update-slice
  10.8 9.5 %all-reduce = s32[48]{0:T(128)S(1)} all-reduce(s32[48]{0:T(128)S(1)} %dynamic-update-slice), channel_id=1, replica_groups=mesh['row'=4,'col'=8] {'col'}, use_global_device_ids=true, to_apply=%add | all-reduce | flops 48 | bytes 384
  20.3 37.3 %all-gather.3.cloned.1.call-done = bf16[8192,128]{1,0:T(8,128)(2,1)} async-done(((bf16[2048,128]{1,0:T(8,128)(2,1)}), bf16[8192,128]{1,0:T(8,128)(2,1)}) %all-gather.3.cloned.1.call-update) | async-done | bytes 2097168 | tf_op jit(solution)/shard_map/all_gather | solution.py:14
  57.6 2.4 %gather_fusion = bf16[48,128,128]{2,1,0:T(8,128)(2,1)S(1)} fusion(bf16[64,128,128]{2,1,0:T(8,128)(2,1)} %bitcast.11, s32[1024]{0:T(1024)S(1)} %pad_clamp_fusion), kind=kCustom, calls=%fused_computation | custom fusion | bytes 3145920 | tf_op jit(solution)/shard_map/gather | solution.py:27
  60.0 23.9 %all-gather.5.cloned.1.call-done = bf16[48,128,128]{2,1,0:T(8,128)(2,1)} async-done(((bf16[6,128,128]{2,1,0:T(8,128)(2,1)}), bf16[48,128,128]{2,1,0:T(8,128)(2,1)}) %all-gather.5.cloned.1.call-update) | async-done | bytes 1572880 | tf_op jit(solution)/shard_map/all_gather | solution.py:19
  83.9 4.3 %convolution_bitcast_fusion = f32[48,128,128]{1,2,0:T(8,128)} fusion(bf16[48,128,128]{2,1,0:T(8,128)(2,1)S(1)} %gather_fusion, bf16[48,128,128]{2,1,0:T(8,128)(2,1)} %all-gather.5.cloned.1.call-done), kind=kOutput, calls=%fused_computation.1 | convolution fusion | flops 201326592 | bytes 6291456 | tf_op jit(solution)/shard_map/sab,sbq->saq/dot_general | solution.py:28
  88.2 2.6 %copy.8 = f32[48,128,128]{2,0,1:T(8,128)S(1)} copy(f32[48,128,128]{1,2,0:T(8,128)} %convolution_bitcast_fusion) | data formatting | bytes 6291456 | tf_op jit(solution)/shard_map/sab,sbq->saq/dot_general | solution.py:28
  90.8 1.2 %fusion.2 = f32[8,128,128]{2,0,1:T(8,128)S(1)} fusion(f32[48,128,128]{2,0,1:T(8,128)S(1)} %copy.8, s32[48]{0:T(128)S(1)} %get-tuple-element.5, pred[48]{0:T(512)(128)(4,1)S(1)} %broadcast_compare_fusion), kind=kOutput, calls=%fused_computation.6 | convolution fusion | flops 75498240 | bytes 3670256 | tf_op jit(solution)/shard_map/sp,saq->paq/dot_general | solution.py:32
  92.0 0.9 copy.9
  (4 shorter events, 0.0 us)
Async XLA Ops:
  6.5 51.1 %all-gather.3.cloned.1.call-start = ((), (), s32[]{:S(2)}) async-start(), calls=%async_computation | async-start | bytes 2621440 | tf_op jit(solution)/shard_map/all_gather | solution.py:14
  7.3 76.7 %all-gather.5.cloned.1.call-start = ((), (), s32[]{:S(2)}) async-start(), calls=%async_computation.1 | async-start | bytes 1769472 | tf_op jit(solution)/shard_map/all_gather | solution.py:19
Sparse Core Ops, SparseCore 0:
  8.9 48.6 all-gather.2
  59.5 24.3 all-gather.4
where the time goes:
time: 99.9 us; the launch traced here: 99.7 us
  waiting for transfers between devices  62.6 us (63%)
  between operations  14.1 us (14%)
  blocking collectives  9.46 us (9%)
  local copies, waits for them, and re-layouts  8.01 us (8%)
  matrix products  5.45 us (5%)
    all_gather x1, waiting for transfers between devices, on_device(): metric_band = lax.all_gather(metric, 'row', axis=0, tiled=True)  37.3 us
    all_gather x1, waiting for transfers between devices, on_device(): piece_slots = lax.all_gather(slots, 'col', axis=0, tiled=True)  23.9 us
    unnamed x1, blocking collectives  9.46 us
    dot_general x1, matrix products, on_device(): jnp.einsum('sab,sbq->saq', piece_slots, rows, preferred_element_type=jnp....  4.29 us
    dot_general x1, local copies, waits for them, and re-layouts, on_device(): jnp.einsum('sab,sbq->saq', piece_slots, rows, preferred_element_type=jnp....  2.58 us
    gather x1, local copies, waits for them, and re-layouts, on_device(): rows = metric_blocks[global_block]  2.44 us
    unnamed x3, local copies, waits for them, and re-layouts  2.1 us
  transfers between devices with their start and end apart: 2, of which 2 were waited for; matrix products, arithmetic and copies ran while one was open for 5% of the time, Pallas kernels for 0%

commit v1 on v0

v1 whole, which is shorter than its diff:
```python
import jax
import jax.numpy as jnp
from jax import lax
from jax.experimental import pallas as pl
from jax.experimental.pallas import tpu as pltpu
from jax.sharding import PartitionSpec as P

PAIR_DEV = 1024
MESH = pl.DeviceIdType.MESH


def kernel(n_row, n_col, list_ref, slots_ref, metric_ref, out_ref, own, held, slots, own_list, lists, table, prev, prod, sems):
    row, col = lax.axis_index("row"), lax.axis_index("col")
    number = list_ref.shape[0]
    halves = len(own)
    col_blocks, width = own[0].shape[0], own[0].shape[1]
    pair_blocks = out_ref.shape[0] // width
    zero = n_col * number

    def has(side, d):
        return row + d < n_row if side == 0 else row - d >= 0

    def toward(side):
        return row - 1 if side == 0 else row + 1

    def peer(d):
        return lax.rem(col + d, n_col)

    barrier = pltpu.get_barrier_semaphore()
    for d in range(1, n_col):
        pl.semaphore_signal(barrier, inc=1, device_id=(row, peer(d)), device_id_type=MESH)
    for side in range(2):

        @pl.when(has(side, 1))
        def _():
            pl.semaphore_signal(barrier, inc=1, device_id=(toward(1 - side), col), device_id_type=MESH)

    lane = lax.broadcasted_iota(jnp.int32, own_list.shape, 1)
    tile = jnp.full(own_list.shape, -1, jnp.int32)
    for s in range(number):
        tile = jnp.where(lane == s, list_ref[s], tile)
    own_list[...] = tile
    prod[zero] = jnp.zeros(prod.shape[1:], prod.dtype)

    near = has(0, 1).astype(jnp.int32) + has(1, 1).astype(jnp.int32)
    pl.semaphore_wait(barrier, n_col - 1 + near)

    def list_copy(d):
        return pltpu.make_async_remote_copy(
            src_ref=own_list, dst_ref=lists.at[col], send_sem=sems["list_send"].at[d], recv_sem=sems["list_recv"].at[d],
            device_id=(row, peer(d)), device_id_type=MESH,
        )

    def slot_copy(d):
        return pltpu.make_async_remote_copy(
            src_ref=slots_ref, dst_ref=slots.at[col], send_sem=sems["slot_send"].at[d], recv_sem=sems["slot_recv"].at[d],
            device_id=(row, peer(d)), device_id_type=MESH,
        )

    def metric_copy(side, d, h):
        source = metric_ref.at[pl.ds(h * col_blocks, col_blocks)] if d == 0 else held[side][d - 1][h]
        return pltpu.make_async_remote_copy(
            src_ref=source, dst_ref=held[side][d][h],
            send_sem=sems["metric_send"].at[side, d, h], recv_sem=sems["metric_recv"].at[side, d, h],
            device_id=(toward(side), col), device_id_type=MESH,
        )

    def own_copy(h):
        return pltpu.make_async_copy(metric_ref.at[pl.ds(h * col_blocks, col_blocks)], own[h], sems["own"].at[h])

    own_slots = pltpu.make_async_copy(slots_ref, slots.at[col], sems["slot_recv"].at[0])
    for d in range(1, n_col):
        list_copy(d).start()
    for h in range(halves):
        for side in range(2):

            @pl.when(has(1 - side, 1))
            def _():
                metric_copy(side, 0, h).start()

    for d in range(1, n_col):
        slot_copy(d).start()
    own_slots.start()
    for h in range(halves):
        own_copy(h).start()

    lists[col] = own_list[...]
    for d in range(1, n_col):
        list_copy(d).wait_recv()
    to_scalars = pltpu.make_async_copy(lists, table, sems["table"].at[0])
    to_scalars.start()
    to_scalars.wait()

    steps = [(0, 0)] + [(side, d) for d in range(1, n_row) for side in range(2)]
    last = [jnp.int32(zero)] * pair_blocks
    for at, (side, d) in enumerate(steps):
        shard = row + d if side == 0 else row - d
        valid = has(side, d)
        shard = jnp.clip(shard, 0, n_row - 1)
        for h in range(halves):
            group = shard * halves + h
            for s in range(number):
                v = table[group, 0, s]
                pair = jnp.where(jnp.logical_and(valid, v >= 0), lax.div(jnp.maximum(v, 0), jnp.int32(col_blocks)), -1)
                before = jnp.int32(zero)
                here = group * number + s
                for p in range(pair_blocks):
                    before = jnp.where(pair == p, last[p], before)
                    last[p] = jnp.where(pair == p, here, last[p])
                prev[(at * halves + h) * number + s] = before

    def forward(d):
        for h in range(halves):
            for side in range(2):

                @pl.when(has(side, d))
                def _():
                    metric_copy(side, d - 1, h).wait_recv()
                    if d < n_row - 1:

                        @pl.when(has(1 - side, 1))
                        def _():
                            metric_copy(side, d, h).start()

    def compute(at):
        side, d = steps[at]
        shard = row + d if side == 0 else row - d

        @pl.when(has(side, d))
        def _():
            for h in range(halves):
                group = shard * halves + h
                rows = own[h] if d == 0 else held[side][d - 1][h]
                if d == 0:
                    own_copy(h).wait()
                arrived = sems["slot_recv"].at[lax.rem(col - group + n_col, n_col)]
                pltpu.make_async_copy(slots_ref, slots.at[group], arrived).wait()
                for s in range(number):
                    v = jnp.maximum(table[group, 0, s], 0)
                    before = prev[(at * halves + h) * number + s]
                    block = rows[lax.rem(v, jnp.int32(col_blocks))]
                    product = jnp.dot(slots[group, s], block, preferred_element_type=jnp.float32)
                    prod[group * number + s] = prod[before] + product

    forward(1)
    compute(0)
    for d in range(1, n_row):
        if d < n_row - 1:
            forward(d + 1)
        compute(2 * d - 1)
        compute(2 * d)

    for p in range(pair_blocks):
        out_ref[pl.ds(p * width, width)] = prod[last[p]]

    for d in range(1, n_col):
        list_copy(d).wait_send()
        slot_copy(d).wait_send()
    for d in range(n_row - 1):
        for h in range(halves):
            for side in range(2):

                @pl.when(jnp.logical_and(has(side, d), has(1 - side, 1)))
                def _():
                    metric_copy(side, d, h).wait_send()


def on_device(slots, block_list, metric):
    n_row, n_col = lax.axis_size("row"), lax.axis_size("col")
    number, width = slots.shape[:2]
    out_cols = metric.shape[1]
    halves = n_col // n_row
    shard_blocks = metric.shape[0] // width
    col_blocks = shard_blocks // halves
    half = pltpu.VMEM((col_blocks, width, out_cols), metric.dtype)
    groups = 2 * n_row - 1
    dma = pltpu.SemaphoreType.DMA
    scratch = [
        [half] * halves,
        [[[half] * halves for _ in range(n_row - 1)] for _ in range(2)],
        pltpu.VMEM((n_col, number, width, width), slots.dtype),
        pltpu.VMEM((8, 128), jnp.int32),
        pltpu.VMEM((n_col, 8, 128), jnp.int32),
        pltpu.SMEM((n_col, 8, 128), jnp.int32),
        pltpu.SMEM((groups * halves * number,), jnp.int32),
        pltpu.VMEM((n_col * number + 1, width, out_cols), jnp.float32),
        {
            "list_send": dma((n_col,)), "list_recv": dma((n_col,)),
            "slot_send": dma((n_col,)), "slot_recv": dma((n_col,)),
            "metric_send": dma((2, n_row - 1, halves)), "metric_recv": dma((2, n_row - 1, halves)),
            "own": dma((halves,)), "table": dma((1,)),
        },
    ]
    flat, tree = jax.tree.flatten(scratch)

    def body(list_ref, slots_ref, metric_ref, out_ref, *refs):
        kernel(n_row, n_col, list_ref, slots_ref, metric_ref, out_ref, *jax.tree.unflatten(tree, refs))

    return pl.pallas_call(
        body,
        out_shape=jax.ShapeDtypeStruct((PAIR_DEV, out_cols), jnp.float32),
        in_specs=[
            pl.BlockSpec(memory_space=pltpu.SMEM),
            pl.BlockSpec(memory_space=pl.ANY),
            pl.BlockSpec(memory_space=pl.ANY),
        ],
        out_specs=pl.BlockSpec(memory_space=pltpu.VMEM),
        scratch_shapes=flat,
        compiler_params=pltpu.CompilerParams(
            collective_id=0, has_side_effects=True, vmem_limit_bytes=40 * 1024 * 1024
        ),
    )(block_list, slots, metric.reshape(shard_blocks, width, out_cols))


def solution(mesh):
    return jax.shard_map(
        on_device,
        mesh=mesh,
        in_specs=(P(("row", "col"), None, None), P(("row", "col")), P("row", "col")),
        out_specs=P("row", "col"),
        check_vma=False,
    )
```

time: 99.9 us -> 45.8 us (0.46)
  waiting for transfers between devices: 62.6 us -> 0 us
  Pallas kernels: 0 us -> 42.2 us
  between operations: 14.1 us -> 0.01 us
  blocking collectives: 9.46 us -> 0 us
  matrix products: 5.45 us -> 0 us
  local copies, waits for them, and re-layouts: 8.01 us -> 3.42 us
    all_gather x2 -> x0, waiting for transfers between devices: 61.2 us -> none  [the longest x1 37.3 us: on_device(): metric_band = lax.all_gather(metric, 'row', axis=0, tiled=True)]
    pallas_call x0 -> x1, Pallas kernels: none -> 42.2 us  [on_device(): pl.pallas_call(body, out_shape=jax.ShapeDtypeStruct((PAIR_DEV, out_cols),...]
    unnamed x1 -> x0, blocking collectives: 9.46 us -> none
    dot_general x2 -> x0, matrix products: 5.45 us -> none  [the longest x1 4.29 us: on_device(): jnp.einsum('sab,sbq->saq', piece_slots, rows, preferred_element_type=jnp....]
    dot_general x2 -> x0, local copies, waits for them, and re-layouts: 3.47 us -> none  [the longest x1 2.58 us: on_device(): jnp.einsum('sab,sbq->saq', piece_slots, rows, preferred_element_type=jnp....]
    gather x1 -> x0, local copies, waits for them, and re-layouts: 2.44 us -> none  [on_device(): rows = metric_blocks[global_block]]
    unnamed x2 -> x0, waiting for transfers between devices: 1.41 us -> none
    unnamed x3 -> x7, local copies, waits for them, and re-layouts: 2.1 us -> 3.42 us
  transfers between devices with their start and end apart: 2 -> 0, of which waited for: 2 -> 0; matrix products, arithmetic and copies ran while one was open for 5% -> 0% of each run, Pallas kernels for 0% -> 0%
where the time goes in v1:
time: 45.8 us; the launch traced here: 45.7 us
  Pallas kernels  42.2 us (92%)
  local copies, waits for them, and re-layouts  3.42 us (7%)
    pallas_call x1, Pallas kernels, on_device(): pl.pallas_call(body, out_shape=jax.ShapeDtypeStruct((PAIR_DEV, out_cols),...  42.2 us
    unnamed x7, local copies, waits for them, and re-layouts  3.42 us

profile of v1, /device:TPU:0, one launch (start us, length us, event | category | flops | bytes accessed | tf_op | source)
XLA Modules:
  0.0 45.7 jit_solution(14000506659326691624)
XLA Ops:
  0.0 0.0 copy-start.2
  0.0 0.7 %copy-done.2 = s32[6]{0:T(128)S(1)} copy-done((s32[6]{0:T(128)S(1)}, s32[6]{0:T(128)}, u32[]{:S(2)}) %copy-start.2) | copy-done | bytes 48
  0.7 0.0 copy-start
  0.7 1.0 %copy-done = bf16[2048,128]{1,0:T(8,128)(2,1)S(1)} copy-done((bf16[2048,128]{1,0:T(8,128)(2,1)S(1)}, bf16[2048,128]{1,0:T(8,128)(2,1)}, u32[]{:S(2)}) %copy-start) | copy-done | bytes 524312
  1.7 0.0 copy-start.1
  1.7 0.9 %copy-done.1 = bf16[6,128,128]{2,1,0:T(8,128)(2,1)S(1)} copy-done((bf16[6,128,128]{2,1,0:T(8,128)(2,1)S(1)}, bf16[6,128,128]{2,1,0:T(8,128)(2,1)}, u32[]{:S(2)}) %copy-start.1) | copy-done | bytes 196632
  2.6 42.2 %shard_map.37 = f32[1024,128]{1,0:T(8,128)S(1)} custom-call(s32[6]{0:T(128)S(1)} %copy-done.2, bf16[6,128,128]{2,1,0:T(8,128)(2,1)S(1)} %copy-done.1, bf16[16,128,128]{2,1,0:T(8,128)(2,1)S(1)} %bitcast.1), custom_call_target="tpu_custom_call" | custom-call | tf_op jit(solution)/shard_map/pallas_call | solution.py:199
  44.9 0.8 %copy.5 = f32[1024,128]{1,0:T(8,128)} copy(f32[1024,128]{1,0:T(8,128)S(1)} %shard_map.37) | data formatting | bytes 1048576
Async XLA Ops:
  0.0 0.7 %copy-start.2 = (s32[6]{0:T(128)S(1)}, s32[6]{0:T(128)}, u32[]{:S(2)}) copy-start(s32[6]{0:T(128)} %list_ref.1) | copy-start | bytes 76
  0.7 1.0 %copy-start = (bf16[2048,128]{1,0:T(8,128)(2,1)S(1)}, bf16[2048,128]{1,0:T(8,128)(2,1)}, u32[]{:S(2)}) copy-start(bf16[2048,128]{1,0:T(8,128)(2,1)} %param.5) | copy-start | bytes 1572868
  1.7 0.9 %copy-start.1 = (bf16[6,128,128]{2,1,0:T(8,128)(2,1)S(1)}, bf16[6,128,128]{2,1,0:T(8,128)(2,1)}, u32[]{:S(2)}) copy-start(bf16[6,128,128]{2,1,0:T(8,128)(2,1)} %slots_ref.1) | copy-start | bytes 589828

commit v2 on v1

--- a/solution.py
+++ b/solution.py
@@ -9,9 +9,10 @@
 MESH = pl.DeviceIdType.MESH
 
 
-def kernel(n_row, n_col, list_ref, slots_ref, metric_ref, out_ref, own, held, slots, own_list, lists, table, prev, prod, sems):
+def kernel(n_row, n_col, list_ref, slots_ref, metric_ref, out_ref, own, held, packed, slots, few, own_list, lists, end_lists, table, end_table, prev, prod, sems):
     row, col = lax.axis_index("row"), lax.axis_index("col")
     number = list_ref.shape[0]
+    pack = packed is not None
     halves = len(own)
     col_blocks, width = own[0].shape[0], own[0].shape[1]
     pair_blocks = out_ref.shape[0] // width
@@ -26,6 +27,18 @@
     def peer(d):
         return lax.rem(col + d, n_col)
 
+    def end(side):
+        return 0 if side == 0 else n_row - 1
+
+    def gate(side):
+        return 1 if side == 0 else n_row - 2
+
+    def is_whole(d, h):
+        return d == 0 and h == 0
+
+    fetch = pltpu.make_async_copy(list_ref, few, sems["table"].at[0])
+    fetch.start()
+
     barrier = pltpu.get_barrier_semaphore()
     for d in range(1, n_col):
         pl.semaphore_signal(barrier, inc=1, device_id=(row, peer(d)), device_id_type=MESH)
@@ -35,20 +48,36 @@
         def _():
             pl.semaphore_signal(barrier, inc=1, device_id=(toward(1 - side), col), device_id_type=MESH)
 
+    expected = n_col - 1 + has(0, 1).astype(jnp.int32) + has(1, 1).astype(jnp.int32)
+    if pack:
+        for side in range(2):
+
+            @pl.when(row == gate(side))
+            def _():
+                for d in range(1, n_col):
+                    pl.semaphore_signal(barrier, inc=1, device_id=(end(side), peer(d)), device_id_type=MESH)
+
+            expected += jnp.where(row == end(side), n_col - 1, 0)
+
+    prod[zero] = jnp.zeros(prod.shape[1:], prod.dtype)
+    fetch.wait()
     lane = lax.broadcasted_iota(jnp.int32, own_list.shape, 1)
     tile = jnp.full(own_list.shape, -1, jnp.int32)
     for s in range(number):
-        tile = jnp.where(lane == s, list_ref[s], tile)
+        tile = jnp.where(lane == s, few[s], tile)
     own_list[...] = tile
-    prod[zero] = jnp.zeros(prod.shape[1:], prod.dtype)
-
-    near = has(0, 1).astype(jnp.int32) + has(1, 1).astype(jnp.int32)
-    pl.semaphore_wait(barrier, n_col - 1 + near)
+    pl.semaphore_wait(barrier, expected)
 
     def list_copy(d):
         return pltpu.make_async_remote_copy(
             src_ref=own_list, dst_ref=lists.at[col], send_sem=sems["list_send"].at[d], recv_sem=sems["list_recv"].at[d],
             device_id=(row, peer(d)), device_id_type=MESH,
+        )
+
+    def end_list_copy(side, d):
+        return pltpu.make_async_remote_copy(
+            src_ref=own_list, dst_ref=end_lists.at[col], send_sem=sems["end_send"].at[d], recv_sem=sems["end_recv"].at[d],
+            device_id=(gate(side), peer(d)), device_id_type=MESH,
         )
 
     def slot_copy(d):
@@ -65,24 +94,82 @@
             device_id=(toward(side), col), device_id_type=MESH,
         )
 
+    def packed_copy(side, d, h):
+        return pltpu.make_async_remote_copy(
+            src_ref=packed[d][h], dst_ref=held[side][d][h].at[pl.ds(0, number)],
+            send_sem=sems["metric_send"].at[side, d, h], recv_sem=sems["metric_recv"].at[side, d, h],
+            device_id=(toward(side), col), device_id_type=MESH,
+        )
+
+    def for_metric(side, d, h, act, to_send):
+        if not pack or is_whole(d, h):
+            act(metric_copy(side, d, h))
+            return
+        at_end = row == (gate(side) if to_send else end(side))
+
+        @pl.when(at_end)
+        def _():
+            act(packed_copy(side, d, h))
+
+        @pl.when(jnp.logical_not(at_end))
+        def _():
+            act(metric_copy(side, d, h))
+
+    def send(side, d, h):
+        if pack and not is_whole(d, h):
+
+            @pl.when(row == gate(side))
+            def _():
+                group = (row + d if side == 0 else row - d) * halves + h
+                rows = own[h] if d == 0 else held[side][d - 1][h]
+                for s in range(number):
+                    v = jnp.maximum(end_table[group, 0, s], 0)
+                    packed[d][h][s] = rows[lax.rem(v, jnp.int32(col_blocks))]
+
+        for_metric(side, d, h, lambda copy: copy.start(), True)
+
     def own_copy(h):
         return pltpu.make_async_copy(metric_ref.at[pl.ds(h * col_blocks, col_blocks)], own[h], sems["own"].at[h])
 
     own_slots = pltpu.make_async_copy(slots_ref, slots.at[col], sems["slot_recv"].at[0])
     for d in range(1, n_col):
         list_copy(d).start()
+    if pack:
+        for side in range(2):
+
+            @pl.when(row == end(side))
+            def _():
+                for d in range(n_col):
+                    end_list_copy(side, d).start()
+
     for h in range(halves):
         for side in range(2):
 
-            @pl.when(has(1 - side, 1))
+            apart = not pack or is_whole(0, h)
+
+            @pl.when(has(1 - side, 1) if apart else jnp.logical_and(has(1 - side, 1), row != gate(side)))
             def _():
                 metric_copy(side, 0, h).start()
 
+    for h in range(halves):
+        own_copy(h).start()
     for d in range(1, n_col):
         slot_copy(d).start()
     own_slots.start()
     for h in range(halves):
-        own_copy(h).start()
+        own_copy(h).wait()
+    if pack:
+        for side in range(2):
+
+            @pl.when(row == gate(side))
+            def _():
+                for d in range(n_col):
+                    end_list_copy(side, d).wait_recv()
+                to_scalars = pltpu.make_async_copy(end_lists, end_table, sems["table"].at[1])
+                to_scalars.start()
+                to_scalars.wait()
+                for h in range(1, halves):
+                    send(side, 0, h)
 
     lists[col] = own_list[...]
     for d in range(1, n_col):
@@ -115,12 +202,12 @@
 
                 @pl.when(has(side, d))
                 def _():
-                    metric_copy(side, d - 1, h).wait_recv()
+                    for_metric(side, d - 1, h, lambda copy: copy.wait_recv(), False)
                     if d < n_row - 1:
 
                         @pl.when(has(1 - side, 1))
                         def _():
-                            metric_copy(side, d, h).start()
+                            send(side, d, h)
 
     def compute(at):
         side, d = steps[at]
@@ -131,14 +218,15 @@
             for h in range(halves):
                 group = shard * halves + h
                 rows = own[h] if d == 0 else held[side][d - 1][h]
-                if d == 0:
-                    own_copy(h).wait()
                 arrived = sems["slot_recv"].at[lax.rem(col - group + n_col, n_col)]
                 pltpu.make_async_copy(slots_ref, slots.at[group], arrived).wait()
                 for s in range(number):
                     v = jnp.maximum(table[group, 0, s], 0)
                     before = prev[(at * halves + h) * number + s]
-                    block = rows[lax.rem(v, jnp.int32(col_blocks))]
+                    at_block = lax.rem(v, jnp.int32(col_blocks))
+                    if pack and d > 0 and not is_whole(d - 1, h):
+                        at_block = jnp.where(row == end(side), s, at_block)
+                    block = rows[at_block]
                     product = jnp.dot(slots[group, s], block, preferred_element_type=jnp.float32)
                     prod[group * number + s] = prod[before] + product
 
@@ -162,7 +250,15 @@
 
                 @pl.when(jnp.logical_and(has(side, d), has(1 - side, 1)))
                 def _():
-                    metric_copy(side, d, h).wait_send()
+                    for_metric(side, d, h, lambda copy: copy.wait_send(), True)
+
+    if pack:
+        for side in range(2):
+
+            @pl.when(row == end(side))
+            def _():
+                for d in range(n_col):
+                    end_list_copy(side, d).wait_send()
 
 
 def on_device(slots, block_list, metric):
@@ -174,13 +270,19 @@
     col_blocks = shard_blocks // halves
     half = pltpu.VMEM((col_blocks, width, out_cols), metric.dtype)
     groups = 2 * n_row - 1
+    pack = n_row >= 4 and number < col_blocks
+    few = pltpu.VMEM((number, width, out_cols), metric.dtype)
     dma = pltpu.SemaphoreType.DMA
     scratch = [
         [half] * halves,
         [[[half] * halves for _ in range(n_row - 1)] for _ in range(2)],
+        [[few] * halves for _ in range(n_row - 1)] if pack else None,
         pltpu.VMEM((n_col, number, width, width), slots.dtype),
+        pltpu.SMEM((number,), jnp.int32),
         pltpu.VMEM((8, 128), jnp.int32),
         pltpu.VMEM((n_col, 8, 128), jnp.int32),
+        pltpu.VMEM((n_col, 8, 128), jnp.int32),
+        pltpu.SMEM((n_col, 8, 128), jnp.int32),
         pltpu.SMEM((n_col, 8, 128), jnp.int32),
         pltpu.SMEM((groups * halves * number,), jnp.int32),
         pltpu.VMEM((n_col * number + 1, width, out_cols), jnp.float32),
@@ -188,7 +290,7 @@
             "list_send": dma((n_col,)), "list_recv": dma((n_col,)),
             "slot_send": dma((n_col,)), "slot_recv": dma((n_col,)),
             "metric_send": dma((2, n_row - 1, halves)), "metric_recv": dma((2, n_row - 1, halves)),
-            "own": dma((halves,)), "table": dma((1,)),
+            "own": dma((halves,)), "table": dma((2,)), "end_send": dma((n_col,)), "end_recv": dma((n_col,)),
         },
     ]
     flat, tree = jax.tree.flatten(scratch)
@@ -200,9 +302,9 @@
         body,
         out_shape=jax.ShapeDtypeStruct((PAIR_DEV, out_cols), jnp.float32),
         in_specs=[
-            pl.BlockSpec(memory_space=pltpu.SMEM),
-            pl.BlockSpec(memory_space=pl.ANY),
-            pl.BlockSpec(memory_space=pl.ANY),
+            pl.BlockSpec(memory_space=pltpu.HBM),
+            pl.BlockSpec(memory_space=pltpu.HBM),
+            pl.BlockSpec(memory_space=pltpu.HBM),
         ],
         out_specs=pl.BlockSpec(memory_space=pltpu.VMEM),
         scratch_shapes=flat,

time: 45.8 us -> 40.6 us (0.89)
  Pallas kernels: 42.2 us -> 36.9 us
    pallas_call x1, Pallas kernels: 42.2 us -> 36.9 us  [on_device(): pl.pallas_call(body, out_shape=jax.ShapeDtypeStruct((PAIR_DEV, out_cols),...]
where the time goes in v2:
time: 40.6 us; the launch traced here: 40.4 us
  Pallas kernels  36.9 us (91%)
  local copies, waits for them, and re-layouts  3.42 us (8%)
    pallas_call x1, Pallas kernels, on_device(): pl.pallas_call(body, out_shape=jax.ShapeDtypeStruct((PAIR_DEV, out_cols),...  36.9 us
    unnamed x7, local copies, waits for them, and re-layouts  3.42 us

profile of v2, /device:TPU:0, one launch (start us, length us, event | category | flops | bytes accessed | tf_op | source)
XLA Modules:
  0.0 40.4 jit_solution(3260375476118201642)
XLA Ops:
  0.0 0.0 copy-start.2
  0.0 0.7 %copy-done.2 = s32[6]{0:T(128)S(1)} copy-done((s32[6]{0:T(128)S(1)}, s32[6]{0:T(128)}, u32[]{:S(2)}) %copy-start.2) | copy-done | bytes 48
  0.7 0.0 copy-start
  0.7 1.0 %copy-done = bf16[2048,128]{1,0:T(8,128)(2,1)S(1)} copy-done((bf16[2048,128]{1,0:T(8,128)(2,1)S(1)}, bf16[2048,128]{1,0:T(8,128)(2,1)}, u32[]{:S(2)}) %copy-start) | copy-done | bytes 524312
  1.7 0.0 copy-start.1
  1.7 0.9 %copy-done.1 = bf16[6,128,128]{2,1,0:T(8,128)(2,1)S(1)} copy-done((bf16[6,128,128]{2,1,0:T(8,128)(2,1)S(1)}, bf16[6,128,128]{2,1,0:T(8,128)(2,1)}, u32[]{:S(2)}) %copy-start.1) | copy-done | bytes 196632
  2.6 36.9 %shard_map.37 = f32[1024,128]{1,0:T(8,128)S(1)} custom-call(s32[6]{0:T(128)S(1)} %copy-done.2, bf16[6,128,128]{2,1,0:T(8,128)(2,1)S(1)} %copy-done.1, bf16[16,128,128]{2,1,0:T(8,128)(2,1)S(1)} %bitcast.1), custom_call_target="tpu_custom_call" | custom-call | tf_op jit(solution)/shard_map/pallas_call | solution.py:301
  39.6 0.8 %copy.5 = f32[1024,128]{1,0:T(8,128)} copy(f32[1024,128]{1,0:T(8,128)S(1)} %shard_map.37) | data formatting | bytes 1048576
Async XLA Ops:
  0.0 0.7 %copy-start.2 = (s32[6]{0:T(128)S(1)}, s32[6]{0:T(128)}, u32[]{:S(2)}) copy-start(s32[6]{0:T(128)} %list_ref.1) | copy-start | bytes 76
  0.7 1.0 %copy-start = (bf16[2048,128]{1,0:T(8,128)(2,1)S(1)}, bf16[2048,128]{1,0:T(8,128)(2,1)}, u32[]{:S(2)}) copy-start(bf16[2048,128]{1,0:T(8,128)(2,1)} %param.5) | copy-start | bytes 1572868
  1.7 0.9 %copy-start.1 = (bf16[6,128,128]{2,1,0:T(8,128)(2,1)S(1)}, bf16[6,128,128]{2,1,0:T(8,128)(2,1)}, u32[]{:S(2)}) copy-start(bf16[6,128,128]{2,1,0:T(8,128)(2,1)} %slots_ref.1) | copy-start | bytes 589828

commit v3 on v2

--- a/solution.py
+++ b/solution.py
@@ -74,6 +74,16 @@
             device_id=(row, peer(d)), device_id_type=MESH,
         )
 
+    sibling = col + 1 - 2 * lax.rem(col, 2)
+
+    def relay_copy(e):
+        source = lax.rem(col - e + n_col, n_col)
+        return pltpu.make_async_remote_copy(
+            src_ref=slots_ref if e == 0 else slots.at[source], dst_ref=slots.at[source],
+            send_sem=sems["slot_send"].at[e + 1], recv_sem=sems["slot_recv"].at[e + 1],
+            device_id=(row, sibling), device_id_type=MESH,
+        )
+
     def end_list_copy(side, d):
         return pltpu.make_async_remote_copy(
             src_ref=own_list, dst_ref=end_lists.at[col], send_sem=sems["end_send"].at[d], recv_sem=sems["end_recv"].at[d],
@@ -153,8 +163,9 @@
 
     for h in range(halves):
         own_copy(h).start()
-    for d in range(1, n_col):
+    for d in range(2, n_col, 2):
         slot_copy(d).start()
+    relay_copy(0).start()
     own_slots.start()
     for h in range(halves):
         own_copy(h).wait()
@@ -180,70 +191,87 @@
 
     steps = [(0, 0)] + [(side, d) for d in range(1, n_row) for side in range(2)]
     last = [jnp.int32(zero)] * pair_blocks
-    for at, (side, d) in enumerate(steps):
-        shard = row + d if side == 0 else row - d
+    turns = [(at, h) for d in range(n_row) for h in range(halves) for at in range(len(steps)) if steps[at][1] == d]
+    for at, h in turns:
+        side, d = steps[at]
         valid = has(side, d)
-        shard = jnp.clip(shard, 0, n_row - 1)
-        for h in range(halves):
-            group = shard * halves + h
-            for s in range(number):
-                v = table[group, 0, s]
-                pair = jnp.where(jnp.logical_and(valid, v >= 0), lax.div(jnp.maximum(v, 0), jnp.int32(col_blocks)), -1)
-                before = jnp.int32(zero)
-                here = group * number + s
-                for p in range(pair_blocks):
-                    before = jnp.where(pair == p, last[p], before)
-                    last[p] = jnp.where(pair == p, here, last[p])
-                prev[(at * halves + h) * number + s] = before
-
-    def forward(d):
-        for h in range(halves):
-            for side in range(2):
-
-                @pl.when(has(side, d))
-                def _():
-                    for_metric(side, d - 1, h, lambda copy: copy.wait_recv(), False)
-                    if d < n_row - 1:
-
-                        @pl.when(has(1 - side, 1))
-                        def _():
-                            send(side, d, h)
-
-    def compute(at):
-        side, d = steps[at]
+        shard = jnp.clip(row + d if side == 0 else row - d, 0, n_row - 1)
+        group = shard * halves + h
+        for s in range(number):
+            v = table[group, 0, s]
+            pair = jnp.where(jnp.logical_and(valid, v >= 0), lax.div(jnp.maximum(v, 0), jnp.int32(col_blocks)), -1)
+            before = jnp.int32(zero)
+            here = group * number + s
+            for p in range(pair_blocks):
+                before = jnp.where(pair == p, last[p], before)
+                last[p] = jnp.where(pair == p, here, last[p])
+            prev[(at * halves + h) * number + s] = before
+
+    def forward(d, h):
+        for side in range(2):
+
+            @pl.when(has(side, d))
+            def _():
+                for_metric(side, d - 1, h, lambda copy: copy.wait_recv(), False)
+                if d < n_row - 1:
+
+                    @pl.when(has(1 - side, 1))
+                    def _():
+                        send(side, d, h)
+
+    def relay():
+        own_slots.wait()
+        for e in range(2, n_col, 2):
+            slot_copy(e).wait_recv()
+            relay_copy(e).start()
+
+    def compute(d, h):
+        for at, (side, distance) in enumerate(steps):
+            if distance == d:
+                compute_side(at, side, d, h)
+
+    def compute_side(at, side, d, h):
         shard = row + d if side == 0 else row - d
 
         @pl.when(has(side, d))
         def _():
-            for h in range(halves):
-                group = shard * halves + h
-                rows = own[h] if d == 0 else held[side][d - 1][h]
-                arrived = sems["slot_recv"].at[lax.rem(col - group + n_col, n_col)]
+            group = shard * halves + h
+            rows = own[h] if d == 0 else held[side][d - 1][h]
+
+            @pl.when(lax.rem(group + col, 2) == 1)
+            def _():
+                arrived = sems["slot_recv"].at[lax.rem(sibling - group + n_col, n_col) + 1]
                 pltpu.make_async_copy(slots_ref, slots.at[group], arrived).wait()
-                for s in range(number):
-                    v = jnp.maximum(table[group, 0, s], 0)
-                    before = prev[(at * halves + h) * number + s]
-                    at_block = lax.rem(v, jnp.int32(col_blocks))
-                    if pack and d > 0 and not is_whole(d - 1, h):
-                        at_block = jnp.where(row == end(side), s, at_block)
-                    block = rows[at_block]
-                    product = jnp.dot(slots[group, s], block, preferred_element_type=jnp.float32)
-                    prod[group * number + s] = prod[before] + product
-
-    forward(1)
-    compute(0)
-    for d in range(1, n_row):
-        if d < n_row - 1:
-            forward(d + 1)
-        compute(2 * d - 1)
-        compute(2 * d)
+
+            for s in range(number):
+                v = jnp.maximum(table[group, 0, s], 0)
+                before = prev[(at * halves + h) * number + s]
+                at_block = lax.rem(v, jnp.int32(col_blocks))
+                if pack and d > 0 and not is_whole(d - 1, h):
+                    at_block = jnp.where(row == end(side), s, at_block)
+                product = jnp.dot(slots[group, s], rows[at_block], preferred_element_type=jnp.float32)
+                prod[group * number + s] = prod[before] + product
+
+    for h in range(halves):
+        forward(1, h)
+    relay()
+    for d in range(2):
+        for h in range(halves):
+            compute(d, h)
+    for d in range(2, n_row):
+        for h in range(halves):
+            forward(d, h)
+            compute(d, h)
 
     for p in range(pair_blocks):
         out_ref[pl.ds(p * width, width)] = prod[last[p]]
 
     for d in range(1, n_col):
         list_copy(d).wait_send()
-        slot_copy(d).wait_send()
+    for d in range(0, n_col, 2):
+        if d > 0:
+            slot_copy(d).wait_send()
+        relay_copy(d).wait_send()
     for d in range(n_row - 1):
         for h in range(halves):
             for side in range(2):
@@ -309,7 +337,7 @@
         out_specs=pl.BlockSpec(memory_space=pltpu.VMEM),
         scratch_shapes=flat,
         compiler_params=pltpu.CompilerParams(
-            collective_id=0, has_side_effects=True, vmem_limit_bytes=40 * 1024 * 1024
+            collective_id=0, has_side_effects=True, vmem_limit_bytes=56 * 1024 * 1024
         ),
     )(block_list, slots, metric.reshape(shard_blocks, width, out_cols))
 

time: 40.6 us -> 39.3 us (0.968)
  local copies, waits for them, and re-layouts: 3.42 us -> 1.87 us
    unnamed x7 -> x1, local copies, waits for them, and re-layouts: 3.42 us -> 1.87 us
where the time goes in v3:
time: 39.3 us; the launch traced here: 39.2 us
  Pallas kernels  37.3 us (95%)
  local copies, waits for them, and re-layouts  1.87 us (5%)
    pallas_call x1, Pallas kernels, on_device(): pl.pallas_call(body, out_shape=jax.ShapeDtypeStruct((PAIR_DEV, out_cols),...  37.3 us
    unnamed x1, local copies, waits for them, and re-layouts  1.87 us

profile of v3, /device:TPU:0, one launch (start us, length us, event | category | flops | bytes accessed | tf_op | source)
XLA Modules:
  0.0 39.2 jit_solution(6106698647176859464)
XLA Ops:
  0.0 37.3 %shard_map.37 = f32[1024,128]{1,0:T(8,128)} custom-call(s32[6]{0:T(128)} %list_ref.1, bf16[6,128,128]{2,1,0:T(8,128)(2,1)} %slots_ref.1, bf16[16,128,128]{2,1,0:T(8,128)(2,1)} %bitcast.1), custom_call_target="tpu_custom_call" | custom-call | tf_op jit(solution)/shard_map/pallas_call | solution.py:329
  37.3 1.9 %copy.5 = f32[1024,128]{1,0:T(8,128)} copy(f32[1024,128]{1,0:T(8,128)} %shard_map.37) | data formatting | bytes 1048576
